TPU v7x, 256 devices: a whole 4x4x8 slice. The times are simulated.
256 devices in a mesh: dp: 64 (over z, x, y_lo), section: 4 (over y_hi, core).
Axes of the slice: x: 4, y: 4 (y_hi: 2, y_lo: 2; y = y_hi * 2 + y_lo), z: 8, core: 2. Of those that a mesh axis runs over, the one named last changes fastest.
Arguments:
- acts: bfloat16 [4, 16384, 1152], P('section', 'dp'), may hold values from -6 to 6
- grad_in: bfloat16 [4, 16384, 1152], P('section', 'dp'), may hold values from -16 to 16
- gain: float32 [4, 1152], P('section'), may hold values from 0.1 to 1.9
- w_in: bfloat16 [4, 1152, 2176], P('section', 'dp'), may hold values from -0.1875 to 0.1875
- w_out: bfloat16 [4, 1152, 2176], P('section', 'dp'), may hold values from -0.125 to 0.125
Outputs:
- handed: bfloat16 [4, 16384, 1152], P('section', 'dp')
- grad_w_in: float32 [4, 1152, 2176], P('section', 'dp')
- grad_w_out: float32 [4, 1152, 2176], P('section', 'dp')
- grad_gain: float32 [4, 1152], P('section')
All inputs are finite; a program needn't handle non-finite values.
Results may differ from a plain program's by a relative error of at most 0.0055.
Values may be sent and summed in bfloat16 or wider, within the bound.
No kernel may reach another device: no remote copies, remote signals or barrier semaphores. Data moves between devices by JAX's collectives and lax.ppermute only.
A program may use at most 128 MiB of HBM per device.

v0:
```python
import jax
import jax.numpy as jnp
from jax import lax
from jax.experimental import pallas as pl
from jax.experimental.pallas import tpu as pltpu
from jax.sharding import Mesh, PartitionSpec as P

coef = 0.7978845608
f32, bf16 = jnp.float32, jnp.bfloat16

SLOTS = (0, 1, 3, 2)
PAD = 40
COST = 200
VMEM = pltpu.CompilerParams(vmem_limit_bytes=56 * 1024 * 1024)


def shift(block, axis, distance):
    size = lax.axis_size(axis)
    return lax.ppermute(block, axis, [(i, (i + distance) % size) for i in range(size)])


def pick(flag, a, b):
    return jnp.where(flag == 0, a, b), jnp.where(flag == 0, b, a)


def ring_gather(block, first, axis, beside):
    size, r = lax.axis_size(axis), block.shape[0]
    me = lax.axis_index(axis)
    out = jnp.zeros((size * r, block.shape[1]), block.dtype)
    out = lax.dynamic_update_slice(out, block, (me * r, 0))
    right, left = first
    for k in range(1, size // 2 + 1):
        if k > 1:
            right, left = after(right, *beside[k - 2]), after(left, *beside[k - 2])
            right, left = shift(right, axis, 1), shift(left, axis, -1)
        out = lax.dynamic_update_slice(out, right, ((me - k) % size * r, 0))
        if k < size - k:
            out = lax.dynamic_update_slice(out, left, ((me + k) % size * r, 0))
    return out


def after(value, *others):
    return lax.optimization_barrier((value,) + others)[0]


def direct_gather(block, axis):
    size = lax.axis_size(axis)
    me = lax.axis_index(axis)
    out = jnp.zeros((size,) + block.shape, block.dtype)
    out = lax.dynamic_update_index_in_dim(out, block, me, 0)
    for k in range(1, size):
        got = shift(block, axis, k)
        out = lax.dynamic_update_index_in_dim(out, got, (me - k) % size, 0)
    return out


def dot(a, b, ca=1, cb=0):
    return lax.dot_general(a, b, (((ca,), (cb,)), ((), ())), preferred_element_type=f32)


TILE = 256


def cuts(width):
    return -(-width // TILE), width % TILE or TILE


def tile_loop(width, body):
    count, last = cuts(width)
    lax.fori_loop(
        0, count - 1, lambda i, _: body(i, pl.ds(pl.multiple_of(i * TILE, TILE), TILE)), None
    )
    body(count - 1, pl.ds((count - 1) * TILE, last))


def start_tiles(width, begin):
    count, last = cuts(width)
    for i in range(count):
        begin(i, pl.ds(i * TILE, TILE if i < count - 1 else last))


def up_kernel(scaled, grads_t, first, slope, out_term, held, slopes, terms, sem):
    width = first.shape[1]

    def load(i, cols):
        return pltpu.make_async_copy(first.at[:, cols], held.at[:, cols], sem.at[0, i])

    def keep(i, cols):
        return pltpu.make_async_copy(slopes.at[:, cols], slope.at[:, cols], sem.at[1, i])

    def send(i, cols):
        return pltpu.make_async_copy(terms.at[:, cols], out_term.at[:, cols], sem.at[2, i])

    def body(i, cols):
        load(i, cols).wait()
        pre = dot(scaled[...], held[:, cols])
        square = pre * pre
        part = 0.5 + 0.5 * jnp.tanh(pre * (coef + (coef * 0.044715) * square))
        slopes[:, cols] = part + part * (1.0 - part) * (
            pre * (2.0 * coef + (2.0 * coef * 0.134145) * square)
        )
        keep(i, cols).start()
        hidden = (pre * part).astype(bf16)
        terms[:, cols] = dot(grads_t[...], hidden).astype(bf16)
        send(i, cols).start()

    def finish(i, cols):
        keep(i, cols).wait()
        send(i, cols).wait()

    start_tiles(width, lambda i, cols: load(i, cols).start())
    tile_loop(width, body)
    start_tiles(width, finish)


def down_kernel(
    place, grads, scaled_t, s0, s1, s2, s3, slope, dpre, o0, o1, o2, o3,
    second, slopes, parts, terms, sem,
):
    rows, width = s0.shape
    ins, outs = (s0, s1, s2, s3), (o0, o1, o2, o3)

    def start(j):
        return pl.multiple_of(place[0, j] * rows, rows)

    def loads(i, cols):
        return [pltpu.make_async_copy(slope.at[:, cols], slopes.at[:, cols], sem.at[4, i])] + [
            pltpu.make_async_copy(
                ins[j].at[:, cols], second.at[pl.ds(start(j), rows), cols], sem.at[j, i]
            )
            for j in range(4)
        ]

    def stores(i, cols):
        return [pltpu.make_async_copy(parts.at[:, cols], dpre.at[:, cols], sem.at[9, i])] + [
            pltpu.make_async_copy(
                terms.at[pl.ds(j * rows, rows), cols], outs[j].at[:, cols], sem.at[5 + j, i]
            )
            for j in range(4)
        ]

    def body(i, cols):
        for copy in loads(i, cols):
            copy.wait()
        parts[:, cols] = (dot(grads[...], second[:, cols]) * slopes[:, cols]).astype(bf16)

        def term(j, _):
            to = pl.ds(pl.multiple_of(j * rows, rows), rows)
            terms[to, cols] = dot(scaled_t[pl.ds(start(j), rows)], parts[:, cols]).astype(bf16)

        lax.fori_loop(0, 4, term, None)
        for copy in stores(i, cols):
            copy.start()

    def begin(i, cols):
        for copy in loads(i, cols):
            copy.start()

    def finish(i, cols):
        for copy in stores(i, cols):
            copy.wait()

    start_tiles(width, begin)
    tile_loop(width, body)
    start_tiles(width, finish)


def back_kernel(dpre, first, scaled, ratio, own, other, gains):
    t, d = scaled.shape
    third = d // 3

    def body(j, _):
        cols = pl.ds(pl.multiple_of(j * third, third), third)
        back = dot(dpre[...], first[cols], 1, 1)
        own[:, cols] = back[: t // 2]
        other[:, cols] = back[t // 2 :].astype(bf16)
        sums = jnp.sum(back * scaled[:, cols].astype(f32), axis=0, keepdims=True)
        gains[:, cols] = sums * ratio[:, cols]

    lax.fori_loop(0, 3, body, None)


WHOLE = pl.BlockSpec(memory_space=pltpu.VMEM)
AWAY = pl.BlockSpec(memory_space=pl.ANY)


def up(scaled, grads_t, first):
    t, d = scaled.shape
    half = first.shape[1]
    return pl.pallas_call(
        up_kernel,
        out_shape=(
            jax.ShapeDtypeStruct((t, half), f32),
            jax.ShapeDtypeStruct((d, half), bf16),
        ),
        in_specs=(WHOLE, WHOLE, AWAY),
        out_specs=(AWAY, AWAY),
        scratch_shapes=[
            pltpu.VMEM((d, half), bf16),
            pltpu.VMEM((t, half), f32),
            pltpu.VMEM((d, half), bf16),
            pltpu.SemaphoreType.DMA((3, cuts(half)[0])),
        ],
        compiler_params=VMEM,
        cost_estimate=pl.CostEstimate(
            flops=4 * t * d * half, bytes_accessed=4 * d * half, transcendentals=t * half
        ),
    )(scaled, grads_t, first)


def down(place, grads, scaled_t, slots, slope):
    t, wide = grads.shape
    rows, half = slots[0].shape
    return pl.pallas_call(
        down_kernel,
        out_shape=(jax.ShapeDtypeStruct((t, half), bf16),)
        + (jax.ShapeDtypeStruct((rows, half), bf16),) * 4,
        in_specs=[pl.BlockSpec(memory_space=pltpu.SMEM), WHOLE, WHOLE] + [AWAY] * 5,
        out_specs=(AWAY,) * 5,
        scratch_shapes=[
            pltpu.VMEM((wide, half), bf16),
            pltpu.VMEM((t, half), f32),
            pltpu.VMEM((t, half), bf16),
            pltpu.VMEM((wide, half), bf16),
            pltpu.SemaphoreType.DMA((10, cuts(half)[0])),
        ],
        compiler_params=VMEM,
        cost_estimate=pl.CostEstimate(
            flops=COST * t * wide * half, bytes_accessed=4 * wide * half, transcendentals=0
        ),
    )(place, grads, scaled_t, *slots, slope)


def back(dpre, first, scaled, ratio):
    t, d = scaled.shape
    half = first.shape[1]
    return pl.pallas_call(
        back_kernel,
        out_shape=(
            jax.ShapeDtypeStruct((t // 2, d), f32),
            jax.ShapeDtypeStruct((t // 2, d), bf16),
            jax.ShapeDtypeStruct((1, d), f32),
        ),
        compiler_params=VMEM,
        cost_estimate=pl.CostEstimate(
            flops=COST * t * d * half, bytes_accessed=4 * d * half, transcendentals=0
        ),
    )(dpre, first, scaled, ratio)


def selector(d, nz, nx):
    rows = d // (nz * nx)
    at = jnp.arange(nx * nz * PAD)
    block, line = at // PAD, at % PAD
    home = (block % nz * nx + block // nz) * rows + line
    home = jnp.where(line < rows, home, -1)
    return (jnp.arange(d)[:, None] == home[None]).astype(bf16)


def local(nz, nx, acts, grad_in, gain, w_in, w_out):
    x, y = lax.axis_index("x"), lax.axis_index("y")
    rows, hid = w_in.shape[1:]
    half = hid // 2
    tokens, d = acts.shape[1:]
    scale = 1.0 / jnp.sqrt(jnp.float32(tokens * nz * nx * 2))

    shards = []
    for w in (w_in[0], w_out[0]):
        mine, theirs = pick(y, w[:, :half], w[:, half:])
        top, bottom = pick(y, mine, shift(theirs, "y", 1))
        shards.append(jnp.concatenate([top, bottom], axis=0))
    block = jnp.pad(shards[1], ((0, PAD - 2 * rows), (0, 0)))
    step = shift(block, "z", 1), shift(block, "z", -1)
    first = direct_gather(shards[0], "x").reshape(nx * 2 * rows, half)
    first = lax.all_gather(after(first, *step), "z", axis=0, tiled=True)

    source = acts[0].astype(f32)
    centred = source - jnp.mean(source, axis=1, keepdims=True)
    inv = 1.0 / jnp.sqrt(jnp.mean(centred * centred, axis=1, keepdims=True) + 1e-06)
    normed = centred * inv
    scaled = (normed * gain[0][None, :]).astype(bf16)
    scaled = jnp.concatenate([scaled, shift(scaled, "y", 1)], axis=0)
    grads = jnp.concatenate([grad_in[0], shift(grad_in[0], "y", 1)], axis=0)
    chosen = selector(d, nz, nx)
    scaled_t = dot(chosen, scaled, 0, 1).astype(bf16)
    grads_w = dot(grads, chosen).astype(bf16)

    second = ring_gather(block, step, "z", [(), (), ()])
    slots = [second] + [shift(second, "x", -o) for o in SLOTS[1:]]
    slope, out_term = up(after(scaled, second, scaled_t, grads_w), grads.T, first)
    sum_out = lax.psum_scatter(out_term, "z", scatter_dimension=0, tiled=True)
    place = jnp.stack([(x + o) % nx for o in SLOTS]).astype(jnp.int32)[None]
    dpre, *terms = down(place, grads_w, scaled_t, slots, slope)
    own, other, grad_g = back(dpre, first, scaled, scale / gain)
    for distance in (1, 2, 4):
        grad_g += shift(grad_g, "z", distance)
    spare = jnp.pad(grad_g.reshape(3, d // 3), ((0, PAD - 2 * rows - 3), (0, half - d // 3)))
    spare = spare.astype(bf16)
    total_in = terms[0].astype(f32)
    for o, term in zip(SLOTS[1:], terms[1:]):
        total_in += shift(term, "x", o).astype(f32)
    sum_out, total_in = lax.optimization_barrier((sum_out, total_in.astype(bf16)))

    spare = jnp.broadcast_to(spare[None], (nx,) + spare.shape)
    sum_out = jnp.concatenate([sum_out.reshape(nx, 2 * rows, half), spare], axis=1)
    total_out = lax.dynamic_index_in_dim(sum_out, x, 0, keepdims=False).astype(f32)
    for o in SLOTS[1:]:
        part = lax.dynamic_index_in_dim(sum_out, (x + o) % nx, 0, keepdims=False)
        total_out += shift(part, "x", o).astype(f32)

    dscaled = own + after(shift(other, "y", 1), total_in).astype(f32)
    dnormed = dscaled * gain[0][None, :]
    grad_x = grad_in[0].astype(f32) + inv * (
        dnormed
        - jnp.mean(dnormed, axis=1, keepdims=True)
        - normed * jnp.mean(dnormed * normed, axis=1, keepdims=True)
    )
    route = [(2 * h + c, (2 * h + c - 1) % 4) for h in range(2) for c in range(2)]
    handed = lax.ppermute(grad_x.astype(bf16), ("h", "c"), route)

    total_in = lax.all_to_all(total_in.reshape(nz, PAD, half), "z", 0, 0)
    total_in = jnp.sum(total_in.astype(f32), axis=0)
    gain_rows = total_out[2 * rows : 2 * rows + 3]

    keeps, sends = zip(
        *(pick(y, w[:rows], w[rows : 2 * rows]) for w in (total_in * scale, total_out * scale))
    )
    got = shift(jnp.concatenate(sends + (gain_rows,), axis=0), "y", 1)
    grad_inw, grad_out = (
        jnp.concatenate(pick(y, keep, got[rows * i : rows * (i + 1)]), axis=1)
        for i, keep in enumerate(keeps)
    )
    grad_g = (gain_rows + got[2 * rows :])[:, : d // 3].reshape(1, d)
    return handed[None], grad_inw[None], grad_out[None], grad_g


def solution(mesh):
    nz, nx = 8, mesh.shape["dp"] // 16
    fine = Mesh(mesh.devices.reshape(nz, nx, 2, 2, 2), ("z", "x", "y", "h", "c"))
    wide = P(("h", "c"), ("z", "x", "y"), None)
    slim = P(("h", "c"), None)

    def run(*args):
        return local(nz, nx, *args)

    return jax.shard_map(
        run,
        mesh=fine,
        in_specs=(wide, wide, slim, wide, wide),
        out_specs=(wide, wide, wide, slim),
        check_vma=False,
    )
```

profile of v0, /device:TPU:10, one launch (start us, length us, event | category | flops | bytes accessed | tf_op | source)
XLA Modules:
  0.0 175.0 jit_solution(16151606810388094986)
XLA Ops:
  21.5 4.0 %collective-permute-start.4 = (bf16[40,1088]{1,0:T(8,128)(2,1)S(1)}, bf16[40,1088]{1,0:T(8,128)(2,1)S(1)}, u32[]{:S(2)}, u32[]{:S(2)}) collective-permute-start(bf16[40,1088]{1,0:T(8,128)(2,1)S(1)} %get-tuple-element.49), channel_id=1, source_target_pairs={{0,224},{32,0},{64,32},{96,64},{128,96},{160,128},{192,160},{224,1... | collective-permute-start | bytes 261128 | tf_op jit(solution)/shard_map/ppermute | solution.py:19
  32.3 3.4 %collective-permute-start.6 = (bf16[40,1088]{1,0:T(8,128)(2,1)S(1)}, bf16[40,1088]{1,0:T(8,128)(2,1)S(1)}, u32[]{:S(2)}, u32[]{:S(2)}) collective-permute-start(bf16[40,1088]{1,0:T(8,128)(2,1)S(1)} %collective-permute-done.4), channel_id=1, source_target_pairs={{0,224},{32,0},{64,32},{96,64},{128,96},{160,128},{192,160},{224,1... | collective-permute-start | bytes 261128 | tf_op jit(solution)/shard_map/ppermute | solution.py:19
  35.7 3.0 %collective-permute-done.5 = bf16[40,1088]{1,0:T(8,128)(2,1)S(1)} collective-permute-done((bf16[40,1088]{1,0:T(8,128)(2,1)S(1)}, bf16[40,1088]{1,0:T(8,128)(2,1)S(1)}, u32[]{:S(2)}, u32[]{:S(2)}) %collective-permute-start.5) | collective-permute-done | bytes 87072 | tf_op jit(solution)/shard_map/ppermute | solution.py:19
  38.7 3.5 %collective-permute-start.8 = (bf16[40,1088]{1,0:T(8,128)(2,1)S(1)}, bf16[40,1088]{1,0:T(8,128)(2,1)S(1)}, u32[]{:S(2)}, u32[]{:S(2)}) collective-permute-start(bf16[40,1088]{1,0:T(8,128)(2,1)S(1)} %collective-permute-done.6), channel_id=1, source_target_pairs={{0,224},{32,0},{64,32},{96,64},{128,96},{160,128},{192,160},{224,1... | collective-permute-start | bytes 261128 | tf_op jit(solution)/shard_map/ppermute | solution.py:19
  42.3 3.3 %collective-permute-done.7 = bf16[40,1088]{1,0:T(8,128)(2,1)S(1)} collective-permute-done((bf16[40,1088]{1,0:T(8,128)(2,1)S(1)}, bf16[40,1088]{1,0:T(8,128)(2,1)S(1)}, u32[]{:S(2)}, u32[]{:S(2)}) %collective-permute-start.7) | collective-permute-done | bytes 87072 | tf_op jit(solution)/shard_map/ppermute | solution.py:19
  45.6 7.4 %collective-permute-done.9 = bf16[40,1088]{1,0:T(8,128)(2,1)S(1)} collective-permute-done((bf16[40,1088]{1,0:T(8,128)(2,1)S(1)}, bf16[40,1088]{1,0:T(8,128)(2,1)S(1)}, u32[]{:S(2)}, u32[]{:S(2)}) %collective-permute-start.9) | collective-permute-done | bytes 87072 | tf_op jit(solution)/shard_map/ppermute | solution.py:19
  54.3 4.5 %collective-permute-start.11 = (bf16[320,1088]{1,0:T(8,128)(2,1)S(1)}, bf16[320,1088]{1,0:T(8,128)(2,1)}, u32[]{:S(2)}, u32[]{:S(2)}) collective-permute-start(bf16[320,1088]{1,0:T(8,128)(2,1)S(1)} %constant_dynamic-update-slice_fusion.s0), channel_id=1, source_target_pairs={{0,8},{8,16},{16,24},{24,0},{1,9},{9,17},{17,25},{25,1},{2,10},{10... | collective-permute-start | bytes 2088968 | tf_op jit(solution)/shard_map/ppermute | solution.py:19
  59.9 3.1 %convolution_convert_fusion.scaled_t = bf16[1280,512]{1,0:T(8,128)(2,1)} fusion(s32[1280]{0:T(1024)S(1)} %fusion.44, bf16[256,1152]{1,0:T(8,128)(2,1)S(1)} %collective-permute-done.1, bf16[256,1152]{1,0:T(8,128)(2,1)S(1)} %fusion.12), kind=kOutput, calls=%fused_computation.3 | convolution fusion | flops 1515913216 | bytes 2495488 | tf_op jit(solution)/shard_map/dot_general | solution.py:58
  64.6 3.0 %fusion.2.grads = bf16[512,1280]{1,0:T(8,128)(2,1)} fusion(s32[1280]{0:T(1024)S(1)} %fusion.44, bf16[256,1152]{1,0:T(8,128)(2,1)S(1)} %collective-permute-done, bf16[256,1152]{1,0:T(8,128)(2,1)S(1)} %bitcast.72), kind=kOutput, calls=%fused_computation.4 | convolution fusion | flops 1514438656 | bytes 2495488 | tf_op jit(solution)/shard_map/dot_general | solution.py:58
  67.6 5.8 %all-gather.2.cloned.1.call-done.first = bf16[1152,1088]{1,0:T(8,128)(2,1)} async-done(((bf16[144,1088]{1,0:T(8,128)(2,1)}), bf16[1152,1088]{1,0:T(8,128)(2,1)}) %all-gather.2.cloned.1.call-update) | async-done | bytes 2506768 | tf_op jit(solution)/shard_map/all_gather | solution.py:275
  73.4 11.3 %shard_map.84 = (f32[512,1088]{1,0:T(8,128)}, bf16[1152,1088]{1,0:T(8,128)(2,1)}) custom-call(bf16[512,1152]{1,0:T(8,128)(2,1)} %pad_maximum_fusion.1.scaled, bf16[1152,512]{1,0:T(8,128)(2,1)} %copy.12.grads_t, bf16[1152,1088]{1,0:T(8,128)(2,1)} %all-gather.2.cloned.1.call-done.first), custom_call_target="tpu_custom_call" | custom-call | flops 2566914048 | bytes 5013504 | tf_op jit(solution)/shard_map/pallas_call | solution.py:190
  84.7 11.7 %shard_map.85 = (bf16[512,1088]{1,0:T(8,128)(2,1)}, bf16[320,1088]{1,0:T(8,128)(2,1)}, bf16[320,1088]{1,0:T(8,128)(2,1)}, bf16[320,1088]{1,0:T(8,128)(2,1)}, bf16[320,1088]{1,0:T(8,128)(2,1)}) custom-call(s32[1,4]{1,0:T(1,128)} %add_bitcast_fusion.place, bf16[512,1280]{1,0:T(8,128)(2,1)} %fusion.2.grads, bf16[1280,512]{1,0:T(8,128)(2,1)} %convolution_convert_fusion.scaled_t, ...), custom_call_target="tpu_custom_call" | custom-call | flops 142606336000 | bytes 5570560 | tf_op jit(solution)/shard_map/pallas_call | solution.py:214
  98.6 2.4 %collective-permute-start.20 = (bf16[320,1088]{1,0:T(8,128)(2,1)}, bf16[320,1088]{1,0:T(8,128)(2,1)}, u32[]{:S(2)}, u32[]{:S(2)}) collective-permute-start(bf16[320,1088]{1,0:T(8,128)(2,1)} %get-tuple-element.29), channel_id=1, source_target_pairs={{0,16},{8,24},{16,0},{24,8},{1,17},{9,25},{17,1},{25,9},{2,18},{10... | collective-permute-start | bytes 2088968 | tf_op jit(solution)/shard_map/ppermute | solution.py:19
  100.9 6.3 %shard_map.86 = (f32[256,1152]{1,0:T(8,128)}, bf16[256,1152]{1,0:T(8,128)(2,1)}, f32[1,1152]{1,0:T(1,128)}) custom-call(bf16[512,1088]{1,0:T(8,128)(2,1)} %get-tuple-element.22.dpre, bf16[1152,1088]{1,0:T(8,128)(2,1)} %all-gather.2.cloned.1.call-done.first, bf16[512,1152]{1,0:T(8,128)(2,1)} %pad_maximum_fusion.1.scaled, f32[1,1152]{1,0:T(1,128)} %get-tuple-element.63.ratio), custom_call_target="tpu_custom_call" | custom-call | flops 128345702400 | bytes 5013504 | tf_op jit(solution)/shard_map/pallas_call | solution.py:237
  108.2 4.1 %collective-permute-done.22 = f32[1,1152]{1,0:T(1,128)S(1)} collective-permute-done((f32[1,1152]{1,0:T(1,128)}, f32[1,1152]{1,0:T(1,128)S(1)}, u32[]{:S(2)}, u32[]{:S(2)}) %collective-permute-start.22) | collective-permute-done | bytes 4640 | tf_op jit(solution)/shard_map/ppermute | solution.py:19
  113.5 5.2 %collective-permute-done.23 = f32[1,1152]{1,0:T(1,128)S(1)} collective-permute-done((f32[1,1152]{1,0:T(1,128)S(1)}, f32[1,1152]{1,0:T(1,128)S(1)}, u32[]{:S(2)}, u32[]{:S(2)}) %collective-permute-start.23) | collective-permute-done | bytes 4640 | tf_op jit(solution)/shard_map/ppermute | solution.py:19
  118.7 2.8 %collective-permute-start.24 = (f32[1,1152]{1,0:T(1,128)S(1)}, f32[1,1152]{1,0:T(1,128)S(1)}, u32[]{:S(2)}, u32[]{:S(2)}) collective-permute-start(f32[1,1152]{1,0:T(1,128)S(1)} %add.269), channel_id=1, source_target_pairs={{0,128},{32,160},{64,192},{96,224},{128,0},{160,32},{192,64},{224,... | collective-permute-start | bytes 13832 | tf_op jit(solution)/shard_map/ppermute | solution.py:19
  122.4 3.9 %collective-permute-done.24 = f32[1,1152]{1,0:T(1,128)S(1)} collective-permute-done((f32[1,1152]{1,0:T(1,128)S(1)}, f32[1,1152]{1,0:T(1,128)S(1)}, u32[]{:S(2)}, u32[]{:S(2)}) %collective-permute-start.24) | collective-permute-done | bytes 4640 | tf_op jit(solution)/shard_map/ppermute | solution.py:19
  126.4 4.4 %collective-permute-done.20 = bf16[320,1088]{1,0:T(8,128)(2,1)} collective-permute-done((bf16[320,1088]{1,0:T(8,128)(2,1)}, bf16[320,1088]{1,0:T(8,128)(2,1)}, u32[]{:S(2)}, u32[]{:S(2)}) %collective-permute-start.20) | collective-permute-done | bytes 696352 | tf_op jit(solution)/shard_map/ppermute | solution.py:19
  130.8 2.3 %add_convert_fusion = bf16[320,1088]{1,0:T(8,128)(2,1)} fusion(bf16[320,1088]{1,0:T(8,128)(2,1)} %collective-permute-done.20, bf16[320,1088]{1,0:T(8,128)(2,1)S(1)} %collective-permute-done.19, bf16[320,1088]{1,0:T(8,128)(2,1)S(1)} %collective-permute-done.18, bf16[320,1088]{1,0:T(8,128)(2,1)S(1)} %copy-done.5), kind=kLoop, calls=%fused_computation.8 | loop fusion | flops 2785280 | bytes 3481600 | tf_op jit(solution)/shard_map/convert_element_type | solution.py:302
  133.2 5.7 %all-to-all-start = ((bf16[8,40,1088]{2,1,0:T(8,128)(2,1)}), bf16[8,40,1088]{2,1,0:T(8,128)(2,1)S(1)}, u32[]{:S(2)}, u32[]{:S(2)}) async-start(bf16[8,40,1088]{2,1,0:T(8,128)(2,1)} %bitcast.15), calls=%async_computation.1 | async-start | bytes 1474560 | tf_op jit(solution)/shard_map/all_to_all | solution.py:321
  142.1 2.9 %collective-permute-start.27 = (bf16[40,1088]{1,0:T(8,128)(2,1)S(1)}, bf16[40,1088]{1,0:T(8,128)(2,1)S(1)}, u32[]{:S(2)}, u32[]{:S(2)}) collective-permute-start(bf16[40,1088]{1,0:T(8,128)(2,1)S(1)} %get-tuple-element.52), channel_id=1, source_target_pairs={{0,16},{8,24},{16,0},{24,8},{1,17},{9,25},{17,1},{25,9},{2,18},{10... | collective-permute-start | bytes 261128 | tf_op jit(solution)/shard_map/ppermute | solution.py:19
  148.6 10.5 %all-to-all-done = bf16[8,40,1088]{2,1,0:T(8,128)(2,1)S(1)} async-done(((bf16[8,40,1088]{2,1,0:T(8,128)(2,1)}), bf16[8,40,1088]{2,1,0:T(8,128)(2,1)S(1)}, u32[]{:S(2)}, u32[]{:S(2)}) %all-to-all-start) | async-done | bytes 696352 | tf_op jit(solution)/shard_map/all_to_all | solution.py:321
  159.7 5.1 %collective-permute-done.28 = f32[39,1088]{1,0:T(8,128)S(1)} collective-permute-done((f32[39,1088]{1,0:T(8,128)S(1)}, f32[39,1088]{1,0:T(8,128)S(1)}, u32[]{:S(2)}, u32[]{:S(2)}) %collective-permute-start.28) | collective-permute-done | bytes 169760 | tf_op jit(solution)/shard_map/ppermute | solution.py:19
  (134 shorter events, 40.9 us)
Async XLA Ops:
  7.2 66.2 %all-gather.2.cloned.1.call-start = ((), (), s32[]{:S(2)}) async-start(), calls=%async_computation.2 | async-start | bytes 2985984 | tf_op jit(solution)/shard_map/all_gather | solution.py:275
  8.2 11.1 %collective-permute-start.2 = (bf16[18,1088]{1,0:T(8,128)(2,1)S(1)}, bf16[18,1088]{1,0:T(8,128)(2,1)S(1)}, u32[]{:S(2)}, u32[]{:S(2)}) collective-permute-start(bf16[18,1088]{1,0:T(8,128)(2,1)S(1)} %broadcast_select_fusion.6), channel_id=1, source_target_pairs={{0,4},{4,0},{1,5},{5,1},{2,6},{6,2},{3,7},{7,3},{8,12},{12,8},{9,1... | collective-permute-start | bytes 117512 | tf_op jit(solution)/shard_map/ppermute | solution.py:19
  15.0 10.5 %collective-permute-start.15 = (bf16[36,1088]{1,0:T(8,128)(2,1)S(1)}, bf16[36,1088]{1,0:T(8,128)(2,1)S(1)}, u32[]{:S(2)}, u32[]{:S(2)}) collective-permute-start(bf16[36,1088]{1,0:T(8,128)(2,1)S(1)} %get-tuple-element.47), channel_id=1, source_target_pairs={{0,16},{8,24},{16,0},{24,8},{1,17},{9,25},{17,1},{25,9},{2,18},{10... | collective-permute-start | bytes 235016 | tf_op jit(solution)/shard_map/ppermute | solution.py:19
  17.2 8.3 %collective-permute-start.14 = (bf16[36,1088]{1,0:T(8,128)(2,1)S(1)}, bf16[36,1088]{1,0:T(8,128)(2,1)S(1)}, u32[]{:S(2)}, u32[]{:S(2)}) collective-permute-start(bf16[36,1088]{1,0:T(8,128)(2,1)S(1)} %get-tuple-element.47), channel_id=1, source_target_pairs={{0,8},{8,16},{16,24},{24,0},{1,9},{9,17},{17,25},{25,1},{2,10},{10... | collective-permute-start | bytes 235016 | tf_op jit(solution)/shard_map/ppermute | solution.py:19
  18.9 6.7 %collective-permute-start.16 = (bf16[36,1088]{1,0:T(8,128)(2,1)S(1)}, bf16[36,1088]{1,0:T(8,128)(2,1)S(1)}, u32[]{:S(2)}, u32[]{:S(2)}) collective-permute-start(bf16[36,1088]{1,0:T(8,128)(2,1)S(1)} %get-tuple-element.47), channel_id=1, source_target_pairs={{0,24},{8,0},{16,8},{24,16},{1,25},{9,1},{17,9},{25,17},{2,26},{10... | collective-permute-start | bytes 235016 | tf_op jit(solution)/shard_map/ppermute | solution.py:19
  19.5 8.5 %collective-permute-start.3 = (bf16[40,1088]{1,0:T(8,128)(2,1)S(1)}, bf16[40,1088]{1,0:T(8,128)(2,1)S(1)}, u32[]{:S(2)}, u32[]{:S(2)}) collective-permute-start(bf16[40,1088]{1,0:T(8,128)(2,1)S(1)} %get-tuple-element.49), channel_id=1, source_target_pairs={{0,32},{32,64},{64,96},{96,128},{128,160},{160,192},{192,224},{224... | collective-permute-start | bytes 261128 | tf_op jit(solution)/shard_map/ppermute | solution.py:19
  28.0 105.1 %reduce-scatter.2.cloned.1.call-start = ((), (), s32[]{:S(2)}) async-start(), calls=%async_computation.3 | async-start | bytes 2985984 | tf_op jit(solution)/shard_map/reduce_scatter | solution.py:291
  29.3 29.5 %collective-permute-start.1 = (bf16[256,1152]{1,0:T(8,128)(2,1)S(1)}, bf16[256,1152]{1,0:T(8,128)(2,1)S(1)}, u32[]{:S(2)}, u32[]{:S(2)}) collective-permute-start(bf16[256,1152]{1,0:T(8,128)(2,1)S(1)} %fusion.12), channel_id=1, source_target_pairs={{0,4},{4,0},{1,5},{5,1},{2,6},{6,2},{3,7},{7,3},{8,12},{12,8},{9,1... | collective-permute-start | bytes 1769480 | tf_op jit(solution)/shard_map/ppermute | solution.py:19
  31.0 32.0 %collective-permute-start = (bf16[256,1152]{1,0:T(8,128)(2,1)S(1)}, bf16[256,1152]{1,0:T(8,128)(2,1)S(1)}, u32[]{:S(2)}, u32[]{:S(2)}) collective-permute-start(bf16[256,1152]{1,0:T(8,128)(2,1)S(1)} %bitcast.70), channel_id=1, source_target_pairs={{0,4},{4,0},{1,5},{5,1},{2,6},{6,2},{3,7},{7,3},{8,12},{12,8},{9,1... | collective-permute-start | bytes 1769480 | tf_op jit(solution)/shard_map/ppermute | solution.py:19
  38.7 6.8 %collective-permute-start.7 = (bf16[40,1088]{1,0:T(8,128)(2,1)S(1)}, bf16[40,1088]{1,0:T(8,128)(2,1)S(1)}, u32[]{:S(2)}, u32[]{:S(2)}) collective-permute-start(bf16[40,1088]{1,0:T(8,128)(2,1)S(1)} %collective-permute-done.5), channel_id=1, source_target_pairs={{0,32},{32,64},{64,96},{96,128},{128,160},{160,192},{192,224},{224... | collective-permute-start | bytes 261128 | tf_op jit(solution)/shard_map/ppermute | solution.py:19
  38.7 6.8 %collective-permute-start.8 = (bf16[40,1088]{1,0:T(8,128)(2,1)S(1)}, bf16[40,1088]{1,0:T(8,128)(2,1)S(1)}, u32[]{:S(2)}, u32[]{:S(2)}) collective-permute-start(bf16[40,1088]{1,0:T(8,128)(2,1)S(1)} %collective-permute-done.6), channel_id=1, source_target_pairs={{0,224},{32,0},{64,32},{96,64},{128,96},{160,128},{192,160},{224,1... | collective-permute-start | bytes 261128 | tf_op jit(solution)/shard_map/ppermute | solution.py:19
  45.5 7.5 %collective-permute-start.9 = (bf16[40,1088]{1,0:T(8,128)(2,1)S(1)}, bf16[40,1088]{1,0:T(8,128)(2,1)S(1)}, u32[]{:S(2)}, u32[]{:S(2)}) collective-permute-start(bf16[40,1088]{1,0:T(8,128)(2,1)S(1)} %collective-permute-done.7), channel_id=1, source_target_pairs={{0,32},{32,64},{64,96},{96,128},{128,160},{160,192},{192,224},{224... | collective-permute-start | bytes 261128 | tf_op jit(solution)/shard_map/ppermute | solution.py:19
  53.0 31.7 %collective-permute-start.12 = (bf16[320,1088]{1,0:T(8,128)(2,1)S(1)}, bf16[320,1088]{1,0:T(8,128)(2,1)}, u32[]{:S(2)}, u32[]{:S(2)}) collective-permute-start(bf16[320,1088]{1,0:T(8,128)(2,1)S(1)} %constant_dynamic-update-slice_fusion.s0), channel_id=1, source_target_pairs={{0,16},{8,24},{16,0},{24,8},{1,17},{9,25},{17,1},{25,9},{2,18},{10... | collective-permute-start | bytes 2088968 | tf_op jit(solution)/shard_map/ppermute | solution.py:19
  54.3 30.4 %collective-permute-start.11 = (bf16[320,1088]{1,0:T(8,128)(2,1)S(1)}, bf16[320,1088]{1,0:T(8,128)(2,1)}, u32[]{:S(2)}, u32[]{:S(2)}) collective-permute-start(bf16[320,1088]{1,0:T(8,128)(2,1)S(1)} %constant_dynamic-update-slice_fusion.s0), channel_id=1, source_target_pairs={{0,8},{8,16},{16,24},{24,0},{1,9},{9,17},{17,25},{25,1},{2,10},{10... | collective-permute-start | bytes 2088968 | tf_op jit(solution)/shard_map/ppermute | solution.py:19
  58.8 25.9 %collective-permute-start.10 = (bf16[320,1088]{1,0:T(8,128)(2,1)S(1)}, bf16[320,1088]{1,0:T(8,128)(2,1)}, u32[]{:S(2)}, u32[]{:S(2)}) collective-permute-start(bf16[320,1088]{1,0:T(8,128)(2,1)S(1)} %constant_dynamic-update-slice_fusion.s0), channel_id=1, source_target_pairs={{0,24},{8,0},{16,8},{24,16},{1,25},{9,1},{17,9},{25,17},{2,26},{10... | collective-permute-start | bytes 2088968 | tf_op jit(solution)/shard_map/ppermute | solution.py:19
  96.5 29.9 %collective-permute-start.18 = (bf16[320,1088]{1,0:T(8,128)(2,1)}, bf16[320,1088]{1,0:T(8,128)(2,1)S(1)}, u32[]{:S(2)}, u32[]{:S(2)}) collective-permute-start(bf16[320,1088]{1,0:T(8,128)(2,1)} %get-tuple-element.27), channel_id=1, source_target_pairs={{0,8},{8,16},{16,24},{24,0},{1,9},{9,17},{17,25},{25,1},{2,10},{10... | collective-permute-start | bytes 2088968 | tf_op jit(solution)/shard_map/ppermute | solution.py:19
  97.5 28.9 %collective-permute-start.19 = (bf16[320,1088]{1,0:T(8,128)(2,1)}, bf16[320,1088]{1,0:T(8,128)(2,1)S(1)}, u32[]{:S(2)}, u32[]{:S(2)}) collective-permute-start(bf16[320,1088]{1,0:T(8,128)(2,1)} %get-tuple-element.28), channel_id=1, source_target_pairs={{0,24},{8,0},{16,8},{24,16},{1,25},{9,1},{17,9},{25,17},{2,26},{10... | collective-permute-start | bytes 2088968 | tf_op jit(solution)/shard_map/ppermute | solution.py:19
  98.6 32.2 %collective-permute-start.20 = (bf16[320,1088]{1,0:T(8,128)(2,1)}, bf16[320,1088]{1,0:T(8,128)(2,1)}, u32[]{:S(2)}, u32[]{:S(2)}) collective-permute-start(bf16[320,1088]{1,0:T(8,128)(2,1)} %get-tuple-element.29), channel_id=1, source_target_pairs={{0,16},{8,24},{16,0},{24,8},{1,17},{9,25},{17,1},{25,9},{2,18},{10... | collective-permute-start | bytes 2088968 | tf_op jit(solution)/shard_map/ppermute | solution.py:19
  118.7 7.6 %collective-permute-start.24 = (f32[1,1152]{1,0:T(1,128)S(1)}, f32[1,1152]{1,0:T(1,128)S(1)}, u32[]{:S(2)}, u32[]{:S(2)}) collective-permute-start(f32[1,1152]{1,0:T(1,128)S(1)} %add.269), channel_id=1, source_target_pairs={{0,128},{32,160},{64,192},{96,224},{128,0},{160,32},{192,64},{224,... | collective-permute-start | bytes 13832 | tf_op jit(solution)/shard_map/ppermute | solution.py:19
  121.6 11.6 %collective-permute-start.17 = (bf16[256,1152]{1,0:T(8,128)(2,1)}, bf16[256,1152]{1,0:T(8,128)(2,1)S(1)}, u32[]{:S(2)}, u32[]{:S(2)}) collective-permute-start(bf16[256,1152]{1,0:T(8,128)(2,1)} %get-tuple-element.24), channel_id=1, source_target_pairs={{0,4},{4,0},{1,5},{5,1},{2,6},{6,2},{3,7},{7,3},{8,12},{12,8},{9,1... | collective-permute-start | bytes 1769480 | tf_op jit(solution)/shard_map/ppermute | solution.py:19
  133.2 25.8 %all-to-all-start = ((bf16[8,40,1088]{2,1,0:T(8,128)(2,1)}), bf16[8,40,1088]{2,1,0:T(8,128)(2,1)S(1)}, u32[]{:S(2)}, u32[]{:S(2)}) async-start(bf16[8,40,1088]{2,1,0:T(8,128)(2,1)} %bitcast.15), calls=%async_computation.1 | async-start | bytes 1474560 | tf_op jit(solution)/shard_map/all_to_all | solution.py:321
  140.0 7.5 %collective-permute-start.25 = (bf16[40,1088]{1,0:T(8,128)(2,1)S(1)}, bf16[40,1088]{1,0:T(8,128)(2,1)S(1)}, u32[]{:S(2)}, u32[]{:S(2)}) collective-permute-start(bf16[40,1088]{1,0:T(8,128)(2,1)S(1)} %get-tuple-element.50), channel_id=1, source_target_pairs={{0,8},{8,16},{16,24},{24,0},{1,9},{9,17},{17,25},{25,1},{2,10},{10... | collective-permute-start | bytes 261128 | tf_op jit(solution)/shard_map/ppermute | solution.py:19
  140.4 7.0 %collective-permute-start.26 = (bf16[40,1088]{1,0:T(8,128)(2,1)S(1)}, bf16[40,1088]{1,0:T(8,128)(2,1)S(1)}, u32[]{:S(2)}, u32[]{:S(2)}) collective-permute-start(bf16[40,1088]{1,0:T(8,128)(2,1)S(1)} %get-tuple-element.51), channel_id=1, source_target_pairs={{0,24},{8,0},{16,8},{24,16},{1,25},{9,1},{17,9},{25,17},{2,26},{10... | collective-permute-start | bytes 261128 | tf_op jit(solution)/shard_map/ppermute | solution.py:19
  147.5 12.2 %collective-permute-start.21 = (bf16[256,1152]{1,0:T(8,128)(2,1)}, bf16[256,1152]{1,0:T(8,128)(2,1)S(1)}, u32[]{:S(2)}, u32[]{:S(2)}) collective-permute-start(bf16[256,1152]{1,0:T(8,128)(2,1)} %fusion.17), channel_id=1, source_target_pairs={{0,3},{1,0},{2,1},{3,2},{4,7},{5,4},{6,5},{7,6},{8,11},{9,8},{10,9... | collective-permute-start | bytes 1769480 | tf_op jit(solution)/shard_map/ppermute | solution.py:319
  (23 other events, 188.1 us)
Sparse Core Ops, SparseCore 0:
  28.1 45.2 all-gather.1
  84.8 43.4 reduce-scatter.1
where the time goes:
time: 176 us; the launch traced here: 175 us
  waiting for transfers between devices  56.5 us (32%)
  starting transfers between devices  48.2 us (27%)
  Pallas kernels  29.3 us (17%)
  between operations  14.5 us (8%)
  other arithmetic  12.9 us (7%)
  local copies, waits for them, and re-layouts  7.39 us (4%)
  matrix products  6.12 us (3%)
    ppermute x28, starting transfers between devices, shift(): lax.ppermute(block, axis, [(i, (i + distance) % size) for i in range(size)])  42.5 us
    ppermute x28, waiting for transfers between devices, shift(): lax.ppermute(block, axis, [(i, (i + distance) % size) for i in range(size)])  40.3 us
    pallas_call x1, Pallas kernels, down(): pl.pallas_call(down_kernel, out_shape=(jax.ShapeDtypeStruct((t, half), bf...  11.7 us
    pallas_call x1, Pallas kernels, up(): pl.pallas_call(up_kernel, out_shape=(jax.ShapeDtypeStruct((t, half), f32)...  11.3 us
    all_to_all x1, waiting for transfers between devices, local(): total_in = lax.all_to_all(total_in.reshape(nz, PAD, half), 'z', 0, 0)  10.5 us
    pallas_call x1, Pallas kernels, back(): pl.pallas_call(back_kernel, out_shape=(jax.ShapeDtypeStruct((t // 2, d),...  6.29 us
    dot_general x2, matrix products, dot(): lax.dot_general(a, b, (((ca,), (cb,)), ((), ())), preferred_element_type=...  6.12 us
    all_gather x1, waiting for transfers between devices, local(): first = lax.all_gather(after(first, *step), 'z', axis=0, tiled=True)  5.77 us
  transfers between devices with their start and end apart: 32, of which 13 were waited for; matrix products, arithmetic and copies ran while one was open for 12% of the time, Pallas kernels for 17%

commit v1 on v0

--- a/solution.py
+++ b/solution.py
@@ -58,7 +58,7 @@
     return lax.dot_general(a, b, (((ca,), (cb,)), ((), ())), preferred_element_type=f32)
 
 
-TILE = 256
+TILE = 512
 
 
 def cuts(width):

time: 176 us -> 174 us (0.989)
  Pallas kernels: 29.3 us -> 25.4 us
    pallas_call x1, Pallas kernels: 11.3 us -> 8.8 us  [up(): pl.pallas_call(up_kernel, out_shape=(jax.ShapeDtypeStruct((t, half), f32)...]
  transfers between devices with their start and end apart: 32 -> 32, of which waited for: 13 -> 14; matrix products, arithmetic and copies ran while one was open for 12% -> 12% of each run, Pallas kernels for 17% -> 15%
where the time goes in v1:
time: 174 us
  waiting for transfers between devices  57.5 us (33%)
  starting transfers between devices  49.9 us (29%)
  Pallas kernels  25.4 us (15%)
  between operations  14.5 us (8%)
  other arithmetic  12.9 us (7%)
  local copies, waits for them, and re-layouts  7.38 us (4%)
  matrix products  6.12 us (4%)
    ppermute x28, starting transfers between devices, shift(): lax.ppermute(block, axis, [(i, (i + distance) % size) for i in range(size)])  44.1 us
    ppermute x28, waiting for transfers between devices, shift(): lax.ppermute(block, axis, [(i, (i + distance) % size) for i in range(size)])  41.1 us
    all_to_all x1, waiting for transfers between devices, local(): total_in = lax.all_to_all(total_in.reshape(nz, PAD, half), 'z', 0, 0)  10.6 us
    pallas_call x1, Pallas kernels, down(): pl.pallas_call(down_kernel, out_shape=(jax.ShapeDtypeStruct((t, half), bf...  10.3 us
    pallas_call x1, Pallas kernels, up(): pl.pallas_call(up_kernel, out_shape=(jax.ShapeDtypeStruct((t, half), f32)...  8.8 us
    pallas_call x1, Pallas kernels, back(): pl.pallas_call(back_kernel, out_shape=(jax.ShapeDtypeStruct((t // 2, d),...  6.27 us
    dot_general x2, matrix products, dot(): lax.dot_general(a, b, (((ca,), (cb,)), ((), ())), preferred_element_type=...  6.12 us
    all_gather x1, waiting for transfers between devices, local(): first = lax.all_gather(after(first, *step), 'z', axis=0, tiled=True)  5.77 us
  transfers between devices with their start and end apart: 32, of which 14 were waited for; matrix products, arithmetic and copies ran while one was open for 12% of the time, Pallas kernels for 15%

profile of v1, /device:TPU:10, one launch (start us, length us, event | category | flops | bytes accessed | tf_op | source)
XLA Modules:
  0.0 173.7 jit_solution(13884748950131048622)
XLA Ops:
  15.0 2.2 %collective-permute-start.15 = (bf16[36,1088]{1,0:T(8,128)(2,1)S(1)}, bf16[36,1088]{1,0:T(8,128)(2,1)S(1)}, u32[]{:S(2)}, u32[]{:S(2)}) collective-permute-start(bf16[36,1088]{1,0:T(8,128)(2,1)S(1)} %get-tuple-element.47), channel_id=1, source_target_pairs={{0,16},{8,24},{16,0},{24,8},{1,17},{9,25},{17,1},{25,9},{2,18},{10... | collective-permute-start | bytes 235016 | tf_op jit(solution)/shard_map/ppermute | solution.py:19
  19.5 2.0 %collective-permute-start.3 = (bf16[40,1088]{1,0:T(8,128)(2,1)S(1)}, bf16[40,1088]{1,0:T(8,128)(2,1)S(1)}, u32[]{:S(2)}, u32[]{:S(2)}) collective-permute-start(bf16[40,1088]{1,0:T(8,128)(2,1)S(1)} %get-tuple-element.49), channel_id=1, source_target_pairs={{0,32},{32,64},{64,96},{96,128},{128,160},{160,192},{192,224},{224... | collective-permute-start | bytes 261128 | tf_op jit(solution)/shard_map/ppermute | solution.py:19
  21.5 4.0 %collective-permute-start.4 = (bf16[40,1088]{1,0:T(8,128)(2,1)S(1)}, bf16[40,1088]{1,0:T(8,128)(2,1)S(1)}, u32[]{:S(2)}, u32[]{:S(2)}) collective-permute-start(bf16[40,1088]{1,0:T(8,128)(2,1)S(1)} %get-tuple-element.49), channel_id=1, source_target_pairs={{0,224},{32,0},{64,32},{96,64},{128,96},{160,128},{192,160},{224,1... | collective-permute-start | bytes 261128 | tf_op jit(solution)/shard_map/ppermute | solution.py:19
  32.3 3.4 %collective-permute-start.6 = (bf16[40,1088]{1,0:T(8,128)(2,1)S(1)}, bf16[40,1088]{1,0:T(8,128)(2,1)S(1)}, u32[]{:S(2)}, u32[]{:S(2)}) collective-permute-start(bf16[40,1088]{1,0:T(8,128)(2,1)S(1)} %collective-permute-done.4), channel_id=1, source_target_pairs={{0,224},{32,0},{64,32},{96,64},{128,96},{160,128},{192,160},{224,1... | collective-permute-start | bytes 261128 | tf_op jit(solution)/shard_map/ppermute | solution.py:19
  35.7 3.0 %collective-permute-done.5 = bf16[40,1088]{1,0:T(8,128)(2,1)S(1)} collective-permute-done((bf16[40,1088]{1,0:T(8,128)(2,1)S(1)}, bf16[40,1088]{1,0:T(8,128)(2,1)S(1)}, u32[]{:S(2)}, u32[]{:S(2)}) %collective-permute-start.5) | collective-permute-done | bytes 87072 | tf_op jit(solution)/shard_map/ppermute | solution.py:19
  38.7 3.5 %collective-permute-start.8 = (bf16[40,1088]{1,0:T(8,128)(2,1)S(1)}, bf16[40,1088]{1,0:T(8,128)(2,1)S(1)}, u32[]{:S(2)}, u32[]{:S(2)}) collective-permute-start(bf16[40,1088]{1,0:T(8,128)(2,1)S(1)} %collective-permute-done.6), channel_id=1, source_target_pairs={{0,224},{32,0},{64,32},{96,64},{128,96},{160,128},{192,160},{224,1... | collective-permute-start | bytes 261128 | tf_op jit(solution)/shard_map/ppermute | solution.py:19
  42.3 3.3 %collective-permute-done.7 = bf16[40,1088]{1,0:T(8,128)(2,1)S(1)} collective-permute-done((bf16[40,1088]{1,0:T(8,128)(2,1)S(1)}, bf16[40,1088]{1,0:T(8,128)(2,1)S(1)}, u32[]{:S(2)}, u32[]{:S(2)}) %collective-permute-start.7) | collective-permute-done | bytes 87072 | tf_op jit(solution)/shard_map/ppermute | solution.py:19
  45.6 7.4 %collective-permute-done.9 = bf16[40,1088]{1,0:T(8,128)(2,1)S(1)} collective-permute-done((bf16[40,1088]{1,0:T(8,128)(2,1)S(1)}, bf16[40,1088]{1,0:T(8,128)(2,1)S(1)}, u32[]{:S(2)}, u32[]{:S(2)}) %collective-permute-start.9) | collective-permute-done | bytes 87072 | tf_op jit(solution)/shard_map/ppermute | solution.py:19
  54.3 4.5 %collective-permute-start.11 = (bf16[320,1088]{1,0:T(8,128)(2,1)S(1)}, bf16[320,1088]{1,0:T(8,128)(2,1)}, u32[]{:S(2)}, u32[]{:S(2)}) collective-permute-start(bf16[320,1088]{1,0:T(8,128)(2,1)S(1)} %constant_dynamic-update-slice_fusion.s0), channel_id=1, source_target_pairs={{0,8},{8,16},{16,24},{24,0},{1,9},{9,17},{17,25},{25,1},{2,10},{10... | collective-permute-start | bytes 2088968 | tf_op jit(solution)/shard_map/ppermute | solution.py:19
  59.9 3.1 %convolution_convert_fusion.scaled_t = bf16[1280,512]{1,0:T(8,128)(2,1)} fusion(s32[1280]{0:T(1024)S(1)} %fusion.44, bf16[256,1152]{1,0:T(8,128)(2,1)S(1)} %collective-permute-done.1, bf16[256,1152]{1,0:T(8,128)(2,1)S(1)} %fusion.12), kind=kOutput, calls=%fused_computation.3 | convolution fusion | flops 1515913216 | bytes 2495488 | tf_op jit(solution)/shard_map/dot_general | solution.py:58
  64.6 3.0 %fusion.2.grads = bf16[512,1280]{1,0:T(8,128)(2,1)} fusion(s32[1280]{0:T(1024)S(1)} %fusion.44, bf16[256,1152]{1,0:T(8,128)(2,1)S(1)} %collective-permute-done, bf16[256,1152]{1,0:T(8,128)(2,1)S(1)} %bitcast.72), kind=kOutput, calls=%fused_computation.4 | convolution fusion | flops 1514438656 | bytes 2495488 | tf_op jit(solution)/shard_map/dot_general | solution.py:58
  67.6 5.8 %all-gather.2.cloned.1.call-done.first = bf16[1152,1088]{1,0:T(8,128)(2,1)} async-done(((bf16[144,1088]{1,0:T(8,128)(2,1)}), bf16[1152,1088]{1,0:T(8,128)(2,1)}) %all-gather.2.cloned.1.call-update) | async-done | bytes 2506768 | tf_op jit(solution)/shard_map/all_gather | solution.py:275
  73.4 8.8 %shard_map.84 = (f32[512,1088]{1,0:T(8,128)}, bf16[1152,1088]{1,0:T(8,128)(2,1)}) custom-call(bf16[512,1152]{1,0:T(8,128)(2,1)} %pad_maximum_fusion.1.scaled, bf16[1152,512]{1,0:T(8,128)(2,1)} %copy.12.grads_t, bf16[1152,1088]{1,0:T(8,128)(2,1)} %all-gather.2.cloned.1.call-done.first), custom_call_target="tpu_custom_call" | custom-call | flops 2566914048 | bytes 5013504 | tf_op jit(solution)/shard_map/pallas_call | solution.py:190
  82.2 10.3 %shard_map.85 = (bf16[512,1088]{1,0:T(8,128)(2,1)}, bf16[320,1088]{1,0:T(8,128)(2,1)}, bf16[320,1088]{1,0:T(8,128)(2,1)}, bf16[320,1088]{1,0:T(8,128)(2,1)}, bf16[320,1088]{1,0:T(8,128)(2,1)}) custom-call(s32[1,4]{1,0:T(1,128)} %add_bitcast_fusion.place, bf16[512,1280]{1,0:T(8,128)(2,1)} %fusion.2.grads, bf16[1280,512]{1,0:T(8,128)(2,1)} %convolution_convert_fusion.scaled_t, ...), custom_call_target="tpu_custom_call" | custom-call | flops 142606336000 | bytes 5570560 | tf_op jit(solution)/shard_map/pallas_call | solution.py:214
  97.3 6.3 %shard_map.86 = (f32[256,1152]{1,0:T(8,128)}, bf16[256,1152]{1,0:T(8,128)(2,1)}, f32[1,1152]{1,0:T(1,128)}) custom-call(bf16[512,1088]{1,0:T(8,128)(2,1)} %get-tuple-element.22.dpre, bf16[1152,1088]{1,0:T(8,128)(2,1)} %all-gather.2.cloned.1.call-done.first, bf16[512,1152]{1,0:T(8,128)(2,1)} %pad_maximum_fusion.1.scaled, f32[1,1152]{1,0:T(1,128)} %get-tuple-element.63.ratio), custom_call_target="tpu_custom_call" | custom-call | flops 128345702400 | bytes 5013504 | tf_op jit(solution)/shard_map/pallas_call | solution.py:237
  104.2 4.4 %collective-permute-done.22 = f32[1,1152]{1,0:T(1,128)S(1)} collective-permute-done((f32[1,1152]{1,0:T(1,128)}, f32[1,1152]{1,0:T(1,128)S(1)}, u32[]{:S(2)}, u32[]{:S(2)}) %collective-permute-start.22) | collective-permute-done | bytes 4640 | tf_op jit(solution)/shard_map/ppermute | solution.py:19
  109.5 5.6 %collective-permute-done.23 = f32[1,1152]{1,0:T(1,128)S(1)} collective-permute-done((f32[1,1152]{1,0:T(1,128)S(1)}, f32[1,1152]{1,0:T(1,128)S(1)}, u32[]{:S(2)}, u32[]{:S(2)}) %collective-permute-start.23) | collective-permute-done | bytes 4640 | tf_op jit(solution)/shard_map/ppermute | solution.py:19
  115.1 4.8 %collective-permute-start.24 = (f32[1,1152]{1,0:T(1,128)S(1)}, f32[1,1152]{1,0:T(1,128)S(1)}, u32[]{:S(2)}, u32[]{:S(2)}) collective-permute-start(f32[1,1152]{1,0:T(1,128)S(1)} %add.269), channel_id=1, source_target_pairs={{0,128},{32,160},{64,192},{96,224},{128,0},{160,32},{192,64},{224,... | collective-permute-start | bytes 13832 | tf_op jit(solution)/shard_map/ppermute | solution.py:19
  122.9 5.7 %collective-permute-done.20 = bf16[320,1088]{1,0:T(8,128)(2,1)} collective-permute-done((bf16[320,1088]{1,0:T(8,128)(2,1)}, bf16[320,1088]{1,0:T(8,128)(2,1)}, u32[]{:S(2)}, u32[]{:S(2)}) %collective-permute-start.20) | collective-permute-done | bytes 696352 | tf_op jit(solution)/shard_map/ppermute | solution.py:19
  128.6 2.3 %add_convert_fusion = bf16[320,1088]{1,0:T(8,128)(2,1)} fusion(bf16[320,1088]{1,0:T(8,128)(2,1)} %collective-permute-done.20, bf16[320,1088]{1,0:T(8,128)(2,1)S(1)} %collective-permute-done.19, bf16[320,1088]{1,0:T(8,128)(2,1)S(1)} %collective-permute-done.18, bf16[320,1088]{1,0:T(8,128)(2,1)S(1)} %copy-done.5), kind=kLoop, calls=%fused_computation.8 | loop fusion | flops 2785280 | bytes 3481600 | tf_op jit(solution)/shard_map/convert_element_type | solution.py:302
  131.7 5.7 %all-to-all-start = ((bf16[8,40,1088]{2,1,0:T(8,128)(2,1)}), bf16[8,40,1088]{2,1,0:T(8,128)(2,1)S(1)}, u32[]{:S(2)}, u32[]{:S(2)}) async-start(bf16[8,40,1088]{2,1,0:T(8,128)(2,1)} %bitcast.15), calls=%async_computation.1 | async-start | bytes 1474560 | tf_op jit(solution)/shard_map/all_to_all | solution.py:321
  140.6 2.9 %collective-permute-start.27 = (bf16[40,1088]{1,0:T(8,128)(2,1)S(1)}, bf16[40,1088]{1,0:T(8,128)(2,1)S(1)}, u32[]{:S(2)}, u32[]{:S(2)}) collective-permute-start(bf16[40,1088]{1,0:T(8,128)(2,1)S(1)} %get-tuple-element.52), channel_id=1, source_target_pairs={{0,16},{8,24},{16,0},{24,8},{1,17},{9,25},{17,1},{25,9},{2,18},{10... | collective-permute-start | bytes 261128 | tf_op jit(solution)/shard_map/ppermute | solution.py:19
  147.1 10.6 %all-to-all-done = bf16[8,40,1088]{2,1,0:T(8,128)(2,1)S(1)} async-done(((bf16[8,40,1088]{2,1,0:T(8,128)(2,1)}), bf16[8,40,1088]{2,1,0:T(8,128)(2,1)S(1)}, u32[]{:S(2)}, u32[]{:S(2)}) %all-to-all-start) | async-done | bytes 696352 | tf_op jit(solution)/shard_map/all_to_all | solution.py:321
  158.2 5.3 %collective-permute-done.28 = f32[39,1088]{1,0:T(8,128)S(1)} collective-permute-done((f32[39,1088]{1,0:T(8,128)S(1)}, f32[39,1088]{1,0:T(8,128)S(1)}, u32[]{:S(2)}, u32[]{:S(2)}) %collective-permute-start.28) | collective-permute-done | bytes 169760 | tf_op jit(solution)/shard_map/ppermute | solution.py:19
  (134 shorter events, 41.2 us)
Async XLA Ops:
  7.2 66.2 %all-gather.2.cloned.1.call-start = ((), (), s32[]{:S(2)}) async-start(), calls=%async_computation.2 | async-start | bytes 2985984 | tf_op jit(solution)/shard_map/all_gather | solution.py:275
  8.2 11.1 %collective-permute-start.2 = (bf16[18,1088]{1,0:T(8,128)(2,1)S(1)}, bf16[18,1088]{1,0:T(8,128)(2,1)S(1)}, u32[]{:S(2)}, u32[]{:S(2)}) collective-permute-start(bf16[18,1088]{1,0:T(8,128)(2,1)S(1)} %broadcast_select_fusion.6), channel_id=1, source_target_pairs={{0,4},{4,0},{1,5},{5,1},{2,6},{6,2},{3,7},{7,3},{8,12},{12,8},{9,1... | collective-permute-start | bytes 117512 | tf_op jit(solution)/shard_map/ppermute | solution.py:19
  15.0 10.5 %collective-permute-start.15 = (bf16[36,1088]{1,0:T(8,128)(2,1)S(1)}, bf16[36,1088]{1,0:T(8,128)(2,1)S(1)}, u32[]{:S(2)}, u32[]{:S(2)}) collective-permute-start(bf16[36,1088]{1,0:T(8,128)(2,1)S(1)} %get-tuple-element.47), channel_id=1, source_target_pairs={{0,16},{8,24},{16,0},{24,8},{1,17},{9,25},{17,1},{25,9},{2,18},{10... | collective-permute-start | bytes 235016 | tf_op jit(solution)/shard_map/ppermute | solution.py:19
  17.2 8.3 %collective-permute-start.14 = (bf16[36,1088]{1,0:T(8,128)(2,1)S(1)}, bf16[36,1088]{1,0:T(8,128)(2,1)S(1)}, u32[]{:S(2)}, u32[]{:S(2)}) collective-permute-start(bf16[36,1088]{1,0:T(8,128)(2,1)S(1)} %get-tuple-element.47), channel_id=1, source_target_pairs={{0,8},{8,16},{16,24},{24,0},{1,9},{9,17},{17,25},{25,1},{2,10},{10... | collective-permute-start | bytes 235016 | tf_op jit(solution)/shard_map/ppermute | solution.py:19
  18.9 6.7 %collective-permute-start.16 = (bf16[36,1088]{1,0:T(8,128)(2,1)S(1)}, bf16[36,1088]{1,0:T(8,128)(2,1)S(1)}, u32[]{:S(2)}, u32[]{:S(2)}) collective-permute-start(bf16[36,1088]{1,0:T(8,128)(2,1)S(1)} %get-tuple-element.47), channel_id=1, source_target_pairs={{0,24},{8,0},{16,8},{24,16},{1,25},{9,1},{17,9},{25,17},{2,26},{10... | collective-permute-start | bytes 235016 | tf_op jit(solution)/shard_map/ppermute | solution.py:19
  19.5 8.5 %collective-permute-start.3 = (bf16[40,1088]{1,0:T(8,128)(2,1)S(1)}, bf16[40,1088]{1,0:T(8,128)(2,1)S(1)}, u32[]{:S(2)}, u32[]{:S(2)}) collective-permute-start(bf16[40,1088]{1,0:T(8,128)(2,1)S(1)} %get-tuple-element.49), channel_id=1, source_target_pairs={{0,32},{32,64},{64,96},{96,128},{128,160},{160,192},{192,224},{224... | collective-permute-start | bytes 261128 | tf_op jit(solution)/shard_map/ppermute | solution.py:19
  28.0 102.9 %reduce-scatter.2.cloned.1.call-start = ((), (), s32[]{:S(2)}) async-start(), calls=%async_computation.3 | async-start | bytes 2985984 | tf_op jit(solution)/shard_map/reduce_scatter | solution.py:291
  29.3 29.5 %collective-permute-start.1 = (bf16[256,1152]{1,0:T(8,128)(2,1)S(1)}, bf16[256,1152]{1,0:T(8,128)(2,1)S(1)}, u32[]{:S(2)}, u32[]{:S(2)}) collective-permute-start(bf16[256,1152]{1,0:T(8,128)(2,1)S(1)} %fusion.12), channel_id=1, source_target_pairs={{0,4},{4,0},{1,5},{5,1},{2,6},{6,2},{3,7},{7,3},{8,12},{12,8},{9,1... | collective-permute-start | bytes 1769480 | tf_op jit(solution)/shard_map/ppermute | solution.py:19
  31.0 32.0 %collective-permute-start = (bf16[256,1152]{1,0:T(8,128)(2,1)S(1)}, bf16[256,1152]{1,0:T(8,128)(2,1)S(1)}, u32[]{:S(2)}, u32[]{:S(2)}) collective-permute-start(bf16[256,1152]{1,0:T(8,128)(2,1)S(1)} %bitcast.70), channel_id=1, source_target_pairs={{0,4},{4,0},{1,5},{5,1},{2,6},{6,2},{3,7},{7,3},{8,12},{12,8},{9,1... | collective-permute-start | bytes 1769480 | tf_op jit(solution)/shard_map/ppermute | solution.py:19
  38.7 6.8 %collective-permute-start.7 = (bf16[40,1088]{1,0:T(8,128)(2,1)S(1)}, bf16[40,1088]{1,0:T(8,128)(2,1)S(1)}, u32[]{:S(2)}, u32[]{:S(2)}) collective-permute-start(bf16[40,1088]{1,0:T(8,128)(2,1)S(1)} %collective-permute-done.5), channel_id=1, source_target_pairs={{0,32},{32,64},{64,96},{96,128},{128,160},{160,192},{192,224},{224... | collective-permute-start | bytes 261128 | tf_op jit(solution)/shard_map/ppermute | solution.py:19
  38.7 6.8 %collective-permute-start.8 = (bf16[40,1088]{1,0:T(8,128)(2,1)S(1)}, bf16[40,1088]{1,0:T(8,128)(2,1)S(1)}, u32[]{:S(2)}, u32[]{:S(2)}) collective-permute-start(bf16[40,1088]{1,0:T(8,128)(2,1)S(1)} %collective-permute-done.6), channel_id=1, source_target_pairs={{0,224},{32,0},{64,32},{96,64},{128,96},{160,128},{192,160},{224,1... | collective-permute-start | bytes 261128 | tf_op jit(solution)/shard_map/ppermute | solution.py:19
  45.5 7.5 %collective-permute-start.9 = (bf16[40,1088]{1,0:T(8,128)(2,1)S(1)}, bf16[40,1088]{1,0:T(8,128)(2,1)S(1)}, u32[]{:S(2)}, u32[]{:S(2)}) collective-permute-start(bf16[40,1088]{1,0:T(8,128)(2,1)S(1)} %collective-permute-done.7), channel_id=1, source_target_pairs={{0,32},{32,64},{64,96},{96,128},{128,160},{160,192},{192,224},{224... | collective-permute-start | bytes 261128 | tf_op jit(solution)/shard_map/ppermute | solution.py:19
  53.0 29.2 %collective-permute-start.12 = (bf16[320,1088]{1,0:T(8,128)(2,1)S(1)}, bf16[320,1088]{1,0:T(8,128)(2,1)}, u32[]{:S(2)}, u32[]{:S(2)}) collective-permute-start(bf16[320,1088]{1,0:T(8,128)(2,1)S(1)} %constant_dynamic-update-slice_fusion.s0), channel_id=1, source_target_pairs={{0,16},{8,24},{16,0},{24,8},{1,17},{9,25},{17,1},{25,9},{2,18},{10... | collective-permute-start | bytes 2088968 | tf_op jit(solution)/shard_map/ppermute | solution.py:19
  54.3 27.9 %collective-permute-start.11 = (bf16[320,1088]{1,0:T(8,128)(2,1)S(1)}, bf16[320,1088]{1,0:T(8,128)(2,1)}, u32[]{:S(2)}, u32[]{:S(2)}) collective-permute-start(bf16[320,1088]{1,0:T(8,128)(2,1)S(1)} %constant_dynamic-update-slice_fusion.s0), channel_id=1, source_target_pairs={{0,8},{8,16},{16,24},{24,0},{1,9},{9,17},{17,25},{25,1},{2,10},{10... | collective-permute-start | bytes 2088968 | tf_op jit(solution)/shard_map/ppermute | solution.py:19
  58.8 23.4 %collective-permute-start.10 = (bf16[320,1088]{1,0:T(8,128)(2,1)S(1)}, bf16[320,1088]{1,0:T(8,128)(2,1)}, u32[]{:S(2)}, u32[]{:S(2)}) collective-permute-start(bf16[320,1088]{1,0:T(8,128)(2,1)S(1)} %constant_dynamic-update-slice_fusion.s0), channel_id=1, source_target_pairs={{0,24},{8,0},{16,8},{24,16},{1,25},{9,1},{17,9},{25,17},{2,26},{10... | collective-permute-start | bytes 2088968 | tf_op jit(solution)/shard_map/ppermute | solution.py:19
  92.5 30.3 %collective-permute-start.18 = (bf16[320,1088]{1,0:T(8,128)(2,1)}, bf16[320,1088]{1,0:T(8,128)(2,1)S(1)}, u32[]{:S(2)}, u32[]{:S(2)}) collective-permute-start(bf16[320,1088]{1,0:T(8,128)(2,1)} %get-tuple-element.27), channel_id=1, source_target_pairs={{0,8},{8,16},{16,24},{24,0},{1,9},{9,17},{17,25},{25,1},{2,10},{10... | collective-permute-start | bytes 2088968 | tf_op jit(solution)/shard_map/ppermute | solution.py:19
  93.6 29.3 %collective-permute-start.19 = (bf16[320,1088]{1,0:T(8,128)(2,1)}, bf16[320,1088]{1,0:T(8,128)(2,1)S(1)}, u32[]{:S(2)}, u32[]{:S(2)}) collective-permute-start(bf16[320,1088]{1,0:T(8,128)(2,1)} %get-tuple-element.28), channel_id=1, source_target_pairs={{0,24},{8,0},{16,8},{24,16},{1,25},{9,1},{17,9},{25,17},{2,26},{10... | collective-permute-start | bytes 2088968 | tf_op jit(solution)/shard_map/ppermute | solution.py:19
  95.4 33.2 %collective-permute-start.20 = (bf16[320,1088]{1,0:T(8,128)(2,1)}, bf16[320,1088]{1,0:T(8,128)(2,1)}, u32[]{:S(2)}, u32[]{:S(2)}) collective-permute-start(bf16[320,1088]{1,0:T(8,128)(2,1)} %get-tuple-element.29), channel_id=1, source_target_pairs={{0,16},{8,24},{16,0},{24,8},{1,17},{9,25},{17,1},{25,9},{2,18},{10... | collective-permute-start | bytes 2088968 | tf_op jit(solution)/shard_map/ppermute | solution.py:19
  115.1 7.6 %collective-permute-start.24 = (f32[1,1152]{1,0:T(1,128)S(1)}, f32[1,1152]{1,0:T(1,128)S(1)}, u32[]{:S(2)}, u32[]{:S(2)}) collective-permute-start(f32[1,1152]{1,0:T(1,128)S(1)} %add.269), channel_id=1, source_target_pairs={{0,128},{32,160},{64,192},{96,224},{128,0},{160,32},{192,64},{224,... | collective-permute-start | bytes 13832 | tf_op jit(solution)/shard_map/ppermute | solution.py:19
  120.0 11.7 %collective-permute-start.17 = (bf16[256,1152]{1,0:T(8,128)(2,1)}, bf16[256,1152]{1,0:T(8,128)(2,1)S(1)}, u32[]{:S(2)}, u32[]{:S(2)}) collective-permute-start(bf16[256,1152]{1,0:T(8,128)(2,1)} %get-tuple-element.24), channel_id=1, source_target_pairs={{0,4},{4,0},{1,5},{5,1},{2,6},{6,2},{3,7},{7,3},{8,12},{12,8},{9,1... | collective-permute-start | bytes 1769480 | tf_op jit(solution)/shard_map/ppermute | solution.py:19
  131.7 26.0 %all-to-all-start = ((bf16[8,40,1088]{2,1,0:T(8,128)(2,1)}), bf16[8,40,1088]{2,1,0:T(8,128)(2,1)S(1)}, u32[]{:S(2)}, u32[]{:S(2)}) async-start(bf16[8,40,1088]{2,1,0:T(8,128)(2,1)} %bitcast.15), calls=%async_computation.1 | async-start | bytes 1474560 | tf_op jit(solution)/shard_map/all_to_all | solution.py:321
  138.5 7.5 %collective-permute-start.25 = (bf16[40,1088]{1,0:T(8,128)(2,1)S(1)}, bf16[40,1088]{1,0:T(8,128)(2,1)S(1)}, u32[]{:S(2)}, u32[]{:S(2)}) collective-permute-start(bf16[40,1088]{1,0:T(8,128)(2,1)S(1)} %get-tuple-element.50), channel_id=1, source_target_pairs={{0,8},{8,16},{16,24},{24,0},{1,9},{9,17},{17,25},{25,1},{2,10},{10... | collective-permute-start | bytes 261128 | tf_op jit(solution)/shard_map/ppermute | solution.py:19
  139.2 6.8 %collective-permute-start.26 = (bf16[40,1088]{1,0:T(8,128)(2,1)S(1)}, bf16[40,1088]{1,0:T(8,128)(2,1)S(1)}, u32[]{:S(2)}, u32[]{:S(2)}) collective-permute-start(bf16[40,1088]{1,0:T(8,128)(2,1)S(1)} %get-tuple-element.51), channel_id=1, source_target_pairs={{0,24},{8,0},{16,8},{24,16},{1,25},{9,1},{17,9},{25,17},{2,26},{10... | collective-permute-start | bytes 261128 | tf_op jit(solution)/shard_map/ppermute | solution.py:19
  146.0 12.2 %collective-permute-start.21 = (bf16[256,1152]{1,0:T(8,128)(2,1)}, bf16[256,1152]{1,0:T(8,128)(2,1)S(1)}, u32[]{:S(2)}, u32[]{:S(2)}) collective-permute-start(bf16[256,1152]{1,0:T(8,128)(2,1)} %fusion.17), channel_id=1, source_target_pairs={{0,3},{1,0},{2,1},{3,2},{4,7},{5,4},{6,5},{7,6},{8,11},{9,8},{10,9... | collective-permute-start | bytes 1769480 | tf_op jit(solution)/shard_map/ppermute | solution.py:319
  (23 other events, 189.5 us)
Sparse Core Ops, SparseCore 0:
  28.1 45.2 all-gather.1
  82.3 43.2 reduce-scatter.1
